TPU v7x, 256 devices: a whole 4x4x8 slice. The times are simulated.
256 devices in a mesh: dp: 32 (over y, z), mp: 8 (over x, core).
Axes of the slice: x: 4, y: 4, z: 8, core: 2. Of those that a mesh axis runs over, the one named last changes fastest.
Arguments:
- activations: bfloat16 [46080, 8192], P('dp', 'mp'), may hold values from -6 to 6
- out_grads: bfloat16 [46080, 2048], P('dp'), may hold values from -0.15625 to 0.15625
- feedback: bfloat16 [32, 8192, 2048], P('dp', 'mp'), may hold values from -6 to 6
- q_prev: float32 [1024, 2, 32], replicated, may hold values from -0.1875 to 0.1875
Outputs:
- error_new: bfloat16 [32, 8192, 2048], P('dp', 'mp')
- q_new: float32 [1024, 2, 32], replicated
All inputs are finite; a program needn't handle non-finite values.
Results may differ from a plain program's by a relative error of at most 0.001.
Values sent between devices are 32-bit elements; how exact they have to be, the bound alone decides.
A program may use at most 128 MiB of HBM per device.

v0:
```python
import jax
import jax.numpy as jnp
from jax import lax
from jax.sharding import PartitionSpec as P


def gram_of(factor_rows):
    return jnp.einsum("dmr,dms->mrs", factor_rows, factor_rows, precision=lax.Precision.HIGHEST)


def orthonormal(factor_rows, factor_low):
    columns = []
    for which in range(factor_rows.shape[1]):
        solved = lax.linalg.triangular_solve(
            factor_low[which],
            factor_rows[:, which, :],
            left_side=False,
            lower=True,
            transpose_a=True,
        )
        columns.append(solved)
    return jnp.stack(columns, axis=1)


def per_device(activations, out_grads, feedback, q_prev):
    highest = lax.Precision.HIGHEST
    n_dp = lax.axis_size("dp")
    kv_width = q_prev.shape[0]
    weight_grad = lax.dot_general(
        activations, out_grads, (((0,), (0,)), ((), ())), preferred_element_type=jnp.float32
    )
    local_rows = weight_grad.shape[0]
    matrix = (weight_grad + feedback[0].astype(jnp.float32)).reshape(local_rows, 2, kv_width)
    p_part = jnp.einsum("dmw,wmr->dmr", matrix, q_prev, precision=highest)
    p_rows = lax.psum(p_part, "dp") / n_dp
    gram_part = gram_of(p_rows)
    gram_sum = lax.psum(gram_part, "mp")
    factor_low = jnp.linalg.cholesky(gram_sum)
    normed = orthonormal(p_rows, factor_low)
    q_part = jnp.einsum("dmw,dmr->wmr", matrix, normed, precision=highest)
    q_new = lax.psum(q_part, ("dp", "mp")) / n_dp
    rebuilt = jnp.einsum("dmr,wmr->dmw", normed, q_new, precision=highest)
    error_new = (matrix - rebuilt).reshape(local_rows, 2 * kv_width).astype(jnp.bfloat16)
    return (error_new[None], q_new)


def solution(mesh):
    return jax.shard_map(
        per_device,
        mesh=mesh,
        in_specs=(P("dp", "mp"), P("dp", None), P("dp", "mp", None), P()),
        out_specs=(P("dp", "mp", None), P()),
        check_vma=False,
    )
```

profile of v0, /device:TPU:1, one launch (start us, length us, event | category | flops | bytes accessed | tf_op | source)
XLA Modules:
  0.0 503.7 jit_solution(904662245819912811)
XLA Ops:
  7.2 0.0 copy-start
  7.2 0.0 all-reduce.3.cloned.1.call-start
  7.2 1.8 copy-done
  9.0 12.3 %convert_add_fusion = f32[1024,2048]{1,0:T(8,128)} fusion(bf16[1,1024,2048]{2,1,0:T(8,128)(2,1)} %param.8, bf16[1440,1024]{1,0:T(8,128)(2,1)S(1)} %copy-done, bf16[1440,2048]{1,0:T(8,128)(2,1)} %param.7), kind=kOutput, calls=%fused_computation | convolution fusion | flops 6043992064 | bytes 21430272 | tf_op jit(solution)/shard_map/dot_general | solution.py:29
  21.3 0.0 copy-start.2
  21.3 9.3 %copy.19 = f32[1024,2048]{0,1:T(8,128)} copy(f32[1024,2048]{1,0:T(8,128)} %convert_add_fusion) | data formatting | bytes 16777216 | tf_op jit(solution)/shard_map/reshape | solution.py:33
  30.6 0.0 copy-done.2
  30.6 8.1 %convolution_bitcast_fusion.1 = f32[1024,2,32]{0,2,1:T(8,128)} fusion(f32[1024,2,1024]{0,2,1:T(8,128)} %bitcast.59, f32[1024,2,32]{0,2,1:T(8,128)S(1)} %copy-done.2), kind=kOutput, calls=%fused_computation.4 | convolution fusion | flops 805306368 | bytes 8912896 | tf_op jit(solution)/shard_map/dmw,wmr->dmr/dot_general | solution.py:34
  38.7 0.0 all-reduce.3.cloned.1.call-update
  38.7 0.0 all-reduce.5.cloned.1.call-start
  38.8 143.6 %all-reduce.3.cloned.1.call-done = f32[1024,2,32]{0,2,1:T(8,128)} async-done(((f32[1024,2,32]{0,2,1:T(8,128)}), f32[1024,2,32]{0,2,1:T(8,128)}) %all-reduce.3.cloned.1.call-update) | async-done | bytes 262160 | tf_op jit(solution)/shard_map/psum | solution.py:35
  182.4 1.4 fusion.10
  183.8 25.3 %psum.22 = f32[2,32,32]{1,2,0:T(8,128)S(1)} all-reduce(f32[2,32,32]{1,2,0:T(8,128)S(1)} %fusion.10), channel_id=1, replica_groups=mesh['dp'=32,'mp'=8] {'mp'}, use_global_device_ids=true, to_apply=%region_1.0 | all-reduce | flops 2048 | bytes 16384 | tf_op jit(solution)/shard_map/psum | solution.py:37
  209.1 0.1 copy.14
  209.2 5.9 %custom-call.7 = f32[2,32,32]{2,1,0:T(8,128)S(1)} custom-call(f32[2,32,32]{2,1,0:T(8,128)S(1)} %fusion.1), custom_call_target="Cholesky" | custom-call | tf_op jit(solution)/shard_map/jit(cholesky)/cholesky | solution.py:38
  215.1 0.1 compare_reduce_fusion
  215.2 0.1 select_select_fusion
  215.3 2.4 custom-call.9
  217.7 2.5 custom-call.10
  220.2 1.0 broadcast_multiply_fusion.1
  221.2 0.3 convolution_bitcast_fusion.3
  221.5 0.3 convolution_bitcast_fusion.2
  221.8 10.6 %convolution_bitcast_fusion = f32[1024,2,32]{0,2,1:T(8,128)} fusion(f32[1024,2,1024]{0,2,1:T(8,128)} %bitcast.60, f32[1024,1,32]{0,2,1:T(8,128)S(1)} %convolution_bitcast_fusion.2, f32[1024,1,32]{0,2,1:T(8,128)S(1)} %convolution_bitcast_fusion.3), kind=kOutput, calls=%fused_computation.3 | convolution fusion | flops 805371904 | bytes 8912896 | tf_op jit(solution)/shard_map/dmw,dmr->wmr/dot_general | solution.py:40
  232.5 0.0 all-reduce.5.cloned.1.call-update
  232.5 246.3 %all-reduce.5.cloned.1.call-done = f32[1024,2,32]{0,2,1:T(8,128)} async-done(((f32[1024,2,32]{0,2,1:T(8,128)}), f32[1024,2,32]{0,2,1:T(8,128)}) %all-reduce.5.cloned.1.call-update) | async-done | bytes 262160 | tf_op jit(solution)/shard_map/psum | solution.py:41
  478.8 1.0 broadcast_multiply_fusion
  479.8 0.0 copy-start.1
  479.8 10.7 %fusion = bf16[1024,2,1024]{0,2,1:T(8,128)(2,1)} fusion(f32[1024,2,1024]{0,2,1:T(8,128)} %bitcast.61, f32[1024,2,32]{0,2,1:T(8,128)S(1)} %broadcast_multiply_fusion, f32[1024,1,32]{0,2,1:T(8,128)S(1)} %convolution_bitcast_fusion.2, f32[1024,1,32]{0,2,1:T(8,128)S(1)} %convolution_bitcast_fusion.3), kind=kOutput, calls=%fused_computation.2 | convolution fusion | flops 809566208 | bytes 13107200 | tf_op jit(solution)/shard_map/dmr,wmr->dmw/dot_general | solution.py:42
  490.5 6.4 %copy.17 = bf16[1,1024,2048]{2,1,0:T(8,128)(2,1)} copy(bf16[1,1024,2048]{1,2,0:T(8,128)(2,1)} %bitcast.62) | data formatting | bytes 8388608
  496.9 0.0 copy-done.1
  (5 shorter events, 0.1 us)
Async XLA Ops:
  7.2 1.8 copy-start
  7.2 175.2 %all-reduce.3.cloned.1.call-start = ((), (), s32[]{:S(2)}) async-start(), calls=%async_computation | async-start | bytes 524288 | tf_op jit(solution)/shard_map/psum | solution.py:35
  21.3 9.3 %copy-start.2 = (f32[1024,2,32]{0,2,1:T(8,128)S(1)}, f32[1024,2,32]{0,2,1:T(8,128)}, u32[]{:S(2)}) copy-start(f32[1024,2,32]{0,2,1:T(8,128)} %param.9) | copy-start | bytes 786436
  38.7 440.1 %all-reduce.5.cloned.1.call-start = ((), (), s32[]{:S(2)}) async-start(), calls=%async_computation.1 | async-start | bytes 524288 | tf_op jit(solution)/shard_map/psum | solution.py:41
  479.8 17.1 %copy-start.1 = (f32[1024,2,32]{0,2,1:T(8,128)}, f32[1024,2,32]{0,2,1:T(8,128)S(1)}, u32[]{:S(2)}) copy-start(f32[1024,2,32]{0,2,1:T(8,128)S(1)} %broadcast_multiply_fusion) | copy-start | bytes 786436
Sparse Core Ops, SparseCore 0:
  38.8 143.4 all-reduce.2
  232.6 246.1 all-reduce.4
where the time goes:
time: 505 us; the launch traced here: 504 us
  waiting for transfers between devices  390 us (77%)
  matrix products  43.7 us (9%)
  blocking collectives  25.3 us (5%)
  local copies, waits for them, and re-layouts  17.6 us (3%)
  between operations  14.1 us (3%)
  other arithmetic  13 us (3%)
    psum x1, waiting for transfers between devices, per_device(): q_new = lax.psum(q_part, ('dp', 'mp')) / n_dp  246 us
    psum x1, waiting for transfers between devices, per_device(): p_rows = lax.psum(p_part, 'dp') / n_dp  144 us
    psum x1, blocking collectives, per_device(): gram_sum = lax.psum(gram_part, 'mp')  25.3 us
    dot_general x1, matrix products, per_device(): lax.dot_general(activations, out_grads, (((0,), (0,)), ((), ())), preferr...  12.3 us
    dot_general x1, matrix products, per_device(): rebuilt = jnp.einsum('dmr,wmr->dmw', normed, q_new, precision=highest)  10.7 us
    dot_general x1, matrix products, per_device(): q_part = jnp.einsum('dmw,dmr->wmr', matrix, normed, precision=highest)  10.6 us
  transfers between devices with their start and end apart: 2, of which 2 were waited for; matrix products, arithmetic and copies ran while one was open for 0% of the time, Pallas kernels for 0%

commit v1 on v0

v1 whole, which is shorter than its diff:
```python
import functools

import jax
import jax.numpy as jnp
from jax import lax
from jax.experimental import pallas as pl
from jax.experimental.pallas import tpu as pltpu
from jax.sharding import PartitionSpec as P

MESH = pl.DeviceIdType.MESH
F32 = jnp.float32
BF16 = jnp.bfloat16
HIGHEST = lax.Precision.HIGHEST

NY, NZ, NX, NC = 4, 8, 4, 2
TOK, ROWS, KVW, R = 1440, 1024, 1024, 32
TOK_PAD = 1536
WIDTH = 2 * KVW
CB = 8
CL = 256
N_PEERS = 31


def ring(step, size):
    return min(step, size - step)


DP_PEERS = sorted(
    [(a, b) for a in range(NY) for b in range(NZ) if (a, b) != (0, 0)],
    key=lambda o: -(ring(o[0], NY) + ring(o[1], NZ)),
)
BLOCK_PEERS = sorted(
    [(a, b, c) for a in range(NY) for b in range(NX) for c in range(NC) if (a, b, c) != (0, 0, 0)],
    key=lambda o: -(ring(o[0], NY) + ring(o[1], NX)),
)
Z_PEERS = sorted(range(1, NZ), key=lambda o: -ring(o, NZ))
MP_PEERS = sorted(
    [(b, c) for b in range(NX) for c in range(NC) if (b, c) != (0, 0)],
    key=lambda o: -ring(o[0], NX),
)


def split3(x):
    hi = x.astype(BF16)
    rest = x - hi.astype(F32)
    mid = rest.astype(BF16)
    low = (rest - mid.astype(F32)).astype(BF16)
    return hi, mid, low


def stack3(x):
    return jnp.concatenate(split3(x), axis=0)


def sum3(x):
    n = x.shape[0] // 3
    return x[:n] + (x[n : 2 * n] + x[2 * n :])


def dot(a, b, ca, cb):
    return lax.dot_general(a, b, (((ca,), (cb,)), ((), ())), preferred_element_type=F32)


def dot_high(a, b, ca, cb):
    return lax.dot_general(
        a, b, (((ca,), (cb,)), ((), ())), precision=HIGHEST, preferred_element_type=F32
    )


def chunk(index):
    row = pl.multiple_of((index // 4) * CB, CB)
    lane = pl.multiple_of(lax.rem(index, 4) * CL, CL)
    return pl.ds(row, CB), pl.ds(lane, CL)


def inverse_factors(gram):
    lane = lax.broadcasted_iota(jnp.int32, (R, 128), 1)
    row = lax.broadcasted_iota(jnp.int32, (R, 128), 0)
    first = lax.rem(lane // R, 2) == 0
    unit = jnp.where(lax.rem(lane, R) == row, 1.0, 0.0).astype(F32)
    w = jnp.where(lane < 2 * R, gram, unit)
    for k in range(R - 1):
        pivot_row = w[k : k + 1, :]
        f0 = w[:, k : k + 1] / pivot_row[:, k : k + 1]
        f1 = w[:, R + k : R + k + 1] / pivot_row[:, R + k : R + k + 1]
        factor = jnp.where(first, f0, f1)
        w = w - jnp.where(row > k, factor * pivot_row, 0.0)
    on0 = jnp.sum(jnp.where(lane == row, w, 0.0), axis=1, keepdims=True)
    on1 = jnp.sum(jnp.where(lane == row + R, w, 0.0), axis=1, keepdims=True)
    w = w * jnp.where(first, 1.0 / jnp.sqrt(on0), 1.0 / jnp.sqrt(on1))
    return w[:, 2 * R : 3 * R], w[:, 3 * R : 4 * R]


def kernel(
    a_hbm, g_hbm, f_hbm, qt_hbm, err_hbm, qn_ref,
    a, g, f, qt, at, mat, mhi, mlo, err, p_part, p_recv, p_full,
    gram_own, gram_recv, q_part, q_recv, z_sum, z_recv, q_full, phat,
    load_sem, out_sem, send_sem, recv_sem,
):
    dp, mp = lax.axis_index("dp"), lax.axis_index("mp")
    y, z, x, c = dp // NZ, lax.rem(dp, NZ), mp // NC, lax.rem(mp, NC)
    block_id = y * 8 + mp

    def dp_target(o):
        return (lax.rem(y + o[0], NY) * NZ + lax.rem(z + o[1], NZ), mp)

    def block_target(o):
        return (
            lax.rem(y + o[0], NY) * NZ + z,
            lax.rem(x + o[1], NX) * NC + lax.rem(c + o[2], NC),
        )

    def z_target(o):
        return (y * NZ + lax.rem(z + o, NZ), mp)

    barrier = pltpu.get_barrier_semaphore()
    greeted = [dp_target(o) for o in DP_PEERS]
    greeted += [block_target(o) for o in BLOCK_PEERS if o[1:] != (0, 0)]
    for target in greeted:
        pl.semaphore_signal(barrier, inc=1, device_id=target, device_id_type=MESH)

    loads = []

    def load(src, dst):
        copy = pltpu.make_async_copy(src, dst, load_sem.at[len(loads)])
        copy.start()
        loads.append(copy)
        return copy

    load_q = load(qt_hbm, qt)
    load_g = [
        load(g_hbm.at[:, pl.ds(m * KVW, KVW)], g.at[pl.ds(0, TOK), pl.ds(m * KVW, KVW)])
        for m in range(2)
    ]
    load_f = [load(f_hbm.at[:, pl.ds(m * KVW, KVW)], f.at[:, pl.ds(m * KVW, KVW)]) for m in range(2)]
    load_a = load(a_hbm, a.at[pl.ds(0, TOK), :])
    g[TOK:, :] = jnp.zeros((TOK_PAD - TOK, WIDTH), BF16)
    a[TOK:, :] = jnp.zeros((TOK_PAD - TOK, ROWS), BF16)

    load_q.wait()
    q3 = [stack3(qt[pl.ds(m * R, R), :]) for m in range(2)]
    inner = []
    for m in range(2):
        load_g[m].wait()
        inner.append(sum3(dot(q3[m], g[:, m * KVW : (m + 1) * KVW], 1, 1)))
    stored = []
    for m in range(2):
        load_f[m].wait()
        stored.append(sum3(dot(q3[m], f[:, m * KVW : (m + 1) * KVW], 1, 1)))
    load_a.wait()
    inner3 = stack3(jnp.concatenate(inner, axis=0))
    p_part[...] = sum3(dot(inner3, a[...], 1, 0)) + jnp.concatenate(stored, axis=0)

    pl.semaphore_wait(barrier, len(greeted))

    def send(src, dst, target, which):
        pltpu.make_async_remote_copy(
            src_ref=src,
            dst_ref=dst,
            send_sem=send_sem.at[which],
            recv_sem=recv_sem.at[which],
            device_id=target,
            device_id_type=MESH,
        ).start()

    def wait_on(sem, view):
        pltpu.make_async_copy(view, view, sem).wait()

    for i, o in enumerate(DP_PEERS):
        target = dp_target(o)
        row, lane = chunk(target[0])
        send(p_part.at[row, lane], p_recv.at[i], target, 0)

    at[...] = a[...].T

    def columns(n):
        lanes = pl.ds(pl.multiple_of(n * 256, 256), 256)
        block = dot(at[...], g[:, lanes], 1, 0) + f[:, lanes].astype(F32)
        mat[:, lanes] = block
        hi = block.astype(BF16)
        mhi[:, lanes] = hi
        mlo[:, lanes] = (block - hi.astype(F32)).astype(BF16)

    pl.loop(0, 4)(columns)

    wait_on(recv_sem.at[0], p_recv)
    row, lane = chunk(dp)
    p_own = p_part[row, lane]
    for i in range(N_PEERS):
        p_own = p_own + p_recv[i]
    p_full[row, lane] = p_own * (1.0 / 32)
    for o in DP_PEERS:
        send(p_full.at[row, lane], p_full.at[row, lane], dp_target(o), 1)

    pl.loop(4, 8)(columns)

    wait_on(recv_sem.at[1], p_recv)
    p_all = p_full[...]

    both = dot_high(p_all, p_all, 1, 1)
    lane64 = lax.broadcasted_iota(jnp.int32, (R, 2 * R), 1)
    terms = jnp.where(lane64 < R, both[:R], both[R:])
    gram_own[...] = jnp.concatenate([terms, jnp.zeros((R, 128 - 2 * R), F32)], axis=1)
    for o in MP_PEERS:
        send(gram_own, gram_recv.at[mp], block_target((0,) + o), 2)
    gram_recv[mp] = gram_own[...]

    for m in range(2):
        cols = slice(m * KVW, (m + 1) * KVW)
        p3 = stack3(p_all[m * R : (m + 1) * R])
        q_part[pl.ds(m * R, R), :] = sum3(dot(p3, mhi[:, cols], 1, 0) + dot(p3, mlo[:, cols], 1, 0))
    for i, o in enumerate(BLOCK_PEERS):
        target = block_target(o)
        row, lane = chunk((target[0] // NZ) * 8 + target[1])
        send(q_part.at[row, lane], q_recv.at[i], target, 3)

    wait_on(recv_sem.at[2], gram_recv.at[pl.ds(0, 7)])
    gram = gram_recv[0]
    for i in range(1, 8):
        gram = gram + gram_recv[i]
    inverses = inverse_factors(gram)

    wait_on(recv_sem.at[3], q_recv)
    row, lane = chunk(block_id)
    q_own = q_part[row, lane]
    for i in range(N_PEERS):
        q_own = q_own + q_recv[i]
    z_sum[...] = q_own
    for o in Z_PEERS:
        send(z_sum, z_recv.at[z], z_target(o), 4)
    z_recv[z] = q_own

    for m in range(2):
        normed = dot_high(inverses[m], p_all[m * R : (m + 1) * R], 1, 0)
        hi, low, _ = split3(normed)
        laid = jnp.concatenate([hi, low, hi, jnp.zeros_like(hi)], axis=0)
        phat[m] = laid.T

    wait_on(recv_sem.at[4], z_recv.at[pl.ds(0, 7)])
    q_own = z_recv[0]
    for i in range(1, NZ):
        q_own = q_own + z_recv[i]
    q_full[row, lane] = q_own * (1.0 / 32)
    for o in BLOCK_PEERS:
        send(q_full.at[row, lane], q_full.at[row, lane], block_target(o), 5)
    wait_on(recv_sem.at[5], q_recv)

    outs = []
    q_new = [dot_high(inverses[m], q_full[m * R : (m + 1) * R, :], 1, 0) for m in range(2)]
    laid = []
    for m in range(2):
        qn_ref[pl.ds(m * R, R), :] = q_new[m]
        hi, low, _ = split3(q_new[m])
        laid.append(jnp.concatenate([hi, hi, low, jnp.zeros_like(hi)], axis=0))
    for i in range(8):
        rows = pl.ds(i * 128, 128)
        for m in range(2):
            cols = slice(m * KVW, (m + 1) * KVW)
            rebuilt = dot(phat[m, rows, :], laid[m], 1, 0)
            err[rows, cols] = (mat[rows, cols] - rebuilt).astype(BF16)
        copy = pltpu.make_async_copy(err.at[rows, :], err_hbm.at[rows, :], out_sem.at[i])
        copy.start()
        outs.append(copy)

    wait_on(send_sem.at[0], p_recv)
    wait_on(send_sem.at[1], p_recv)
    wait_on(send_sem.at[2], gram_recv.at[pl.ds(0, 7)])
    wait_on(send_sem.at[3], q_recv)
    wait_on(send_sem.at[4], z_recv.at[pl.ds(0, 7)])
    wait_on(send_sem.at[5], q_recv)
    for copy in outs:
        copy.wait()


def per_device(activations, out_grads, feedback, q_prev):
    qt = jnp.transpose(q_prev, (1, 2, 0)).reshape(2 * R, KVW)
    any_space = pl.BlockSpec(memory_space=pl.ANY)
    err, qn = pl.pallas_call(
        kernel,
        out_shape=(
            jax.ShapeDtypeStruct((ROWS, WIDTH), BF16),
            jax.ShapeDtypeStruct((2 * R, KVW), F32),
        ),
        in_specs=[any_space] * 4,
        out_specs=(any_space, pl.BlockSpec(memory_space=pltpu.VMEM)),
        scratch_shapes=[
            pltpu.VMEM((TOK_PAD, ROWS), BF16),
            pltpu.VMEM((TOK_PAD, WIDTH), BF16),
            pltpu.VMEM((ROWS, WIDTH), BF16),
            pltpu.VMEM((2 * R, KVW), F32),
            pltpu.VMEM((ROWS, TOK_PAD), BF16),
            pltpu.VMEM((ROWS, WIDTH), F32),
            pltpu.VMEM((ROWS, WIDTH), BF16),
            pltpu.VMEM((ROWS, WIDTH), BF16),
            pltpu.VMEM((ROWS, WIDTH), BF16),
            pltpu.VMEM((2 * R, ROWS), F32),
            pltpu.VMEM((N_PEERS, CB, CL), F32),
            pltpu.VMEM((2 * R, ROWS), F32),
            pltpu.VMEM((R, 128), F32),
            pltpu.VMEM((8, R, 128), F32),
            pltpu.VMEM((2 * R, KVW), F32),
            pltpu.VMEM((N_PEERS, CB, CL), F32),
            pltpu.VMEM((CB, CL), F32),
            pltpu.VMEM((NZ, CB, CL), F32),
            pltpu.VMEM((2 * R, KVW), F32),
            pltpu.VMEM((2, ROWS, 128), BF16),
            pltpu.SemaphoreType.DMA((6,)),
            pltpu.SemaphoreType.DMA((8,)),
            pltpu.SemaphoreType.DMA((6,)),
            pltpu.SemaphoreType.DMA((6,)),
        ],
        compiler_params=pltpu.CompilerParams(
            collective_id=0, has_side_effects=True, vmem_limit_bytes=60 * 2**20
        ),
    )(activations, out_grads, feedback[0], qt)
    q_new = jnp.transpose(qn.reshape(2, R, KVW), (2, 0, 1))
    return err[None], q_new


def solution(mesh):
    return jax.shard_map(
        per_device,
        mesh=mesh,
        in_specs=(P("dp", "mp"), P("dp", None), P("dp", "mp", None), P()),
        out_specs=(P("dp", "mp", None), P()),
        check_vma=False,
    )
```

time: 505 us -> 57.8 us (0.11)
  waiting for transfers between devices: 390 us -> 0 us
  Pallas kernels: 0 us -> 51.5 us
  matrix products: 43.7 us -> 0 us
  blocking collectives: 25.3 us -> 0 us
  between operations: 14.1 us -> 0.65 us
  other arithmetic: 13 us -> 0 us
  local copies, waits for them, and re-layouts: 17.6 us -> 5.54 us
    psum x2 -> x0, waiting for transfers between devices: 390 us -> none  [the longest x1 246 us: per_device(): q_new = lax.psum(q_part, ('dp', 'mp')) / n_dp]
    pallas_call x0 -> x1, Pallas kernels: none -> 51.5 us  [per_device(): pl.pallas_call(kernel, out_shape=(jax.ShapeDtypeStruct((ROWS, WIDTH), BF1...]
    dot_general x5 -> x0, matrix products: 43.1 us -> none  [the longest x1 12.3 us: per_device(): lax.dot_general(activations, out_grads, (((0,), (0,)), ((), ())), preferr...]
    psum x1 -> x0, blocking collectives: 25.3 us -> none  [per_device(): gram_sum = lax.psum(gram_part, 'mp')]
    another operation x8 -> x0, other arithmetic: 10.9 us -> none  [the longest x4 6.03 us: per_device(): factor_low = jnp.linalg.cholesky(gram_sum)]
    reshape x1 -> x0, local copies, waits for them, and re-layouts: 9.32 us -> none  [per_device(): (weight_grad + feedback[0].astype(jnp.float32)).reshape(local_rows, 2, kv...]
  transfers between devices with their start and end apart: 2 -> 0, of which waited for: 2 -> 0; matrix products, arithmetic and copies ran while one was open for 0% -> 0% of each run, Pallas kernels for 0% -> 0%
where the time goes in v1:
time: 57.8 us; the launch traced here: 57.7 us
  Pallas kernels  51.5 us (89%)
  local copies, waits for them, and re-layouts  5.54 us (10%)
  between operations  0.65 us (1%)
    pallas_call x1, Pallas kernels, per_device(): pl.pallas_call(kernel, out_shape=(jax.ShapeDtypeStruct((ROWS, WIDTH), BF1...  51.5 us
    unnamed x4, local copies, waits for them, and re-layouts  5.54 us

profile of v1, /device:TPU:1, one launch (start us, length us, event | category | flops | bytes accessed | tf_op | source)
XLA Modules:
  0.0 57.7 jit_solution(4192871728646669439)
XLA Ops:
  0.6 51.5 %shard_map.59 = (bf16[1024,2048]{1,0:T(8,128)(2,1)}, f32[64,1024]{1,0:T(8,128)}) custom-call(bf16[1440,1024]{1,0:T(8,128)(2,1)} %a_hbm.1, bf16[1440,2048]{1,0:T(8,128)(2,1)} %g_hbm.1, bf16[1024,2048]{1,0:T(8,128)(2,1)} %bitcast.8, f32[64,1024]{1,0:T(8,128)} %bitcast.10), custom_call_target="tpu_custom_call" | custom-call | tf_op jit(solution)/shard_map/pallas_call | solution.py:278
  52.1 0.0 copy-start
  52.1 4.8 %copy.8 = bf16[1,1024,2048]{2,1,0:T(8,128)(2,1)} copy(bf16[1,1024,2048]{2,1,0:T(8,128)(2,1)} %bitcast.9) | data formatting | bytes 8388608
  57.0 0.0 copy-done
  57.0 0.7 %copy.9 = f32[1024,2,32]{0,2,1:T(8,128)} copy(f32[1024,2,32]{0,2,1:T(8,128)S(1)} %bitcast.11) | data formatting | bytes 524288
Async XLA Ops:
  52.1 4.8 %copy-start = (f32[64,1024]{1,0:T(8,128)S(1)}, f32[64,1024]{1,0:T(8,128)}, u32[]{:S(2)}) copy-start(f32[64,1024]{1,0:T(8,128)} %get-tuple-element.5) | copy-start | bytes 786436

commit v2 on v1

v2 whole, which is shorter than its diff:
```python
import functools

import jax
import jax.numpy as jnp
from jax import lax
from jax.experimental import pallas as pl
from jax.experimental.pallas import tpu as pltpu
from jax.sharding import PartitionSpec as P

MESH = pl.DeviceIdType.MESH
F32 = jnp.float32
BF16 = jnp.bfloat16
HIGHEST = lax.Precision.HIGHEST

NY, NZ, NX, NC = 4, 8, 4, 2
TOK, ROWS, KVW, R = 1440, 1024, 1024, 32
TOK_PAD = 1536
WIDTH = 2 * KVW
CB = 8
CL = 128
N_PEERS = 31


def ring(step, size):
    return min(step, size - step)


DP_PEERS = sorted(
    [(a, b) for a in range(NY) for b in range(NZ) if (a, b) != (0, 0)],
    key=lambda o: -(ring(o[0], NY) + ring(o[1], NZ)),
)
BLOCK_PEERS = sorted(
    [(a, b, c) for a in range(NY) for b in range(NX) for c in range(NC) if (a, b, c) != (0, 0, 0)],
    key=lambda o: -(ring(o[0], NY) + ring(o[1], NX)),
)
Z_PEERS = sorted(range(1, NZ), key=lambda o: -ring(o, NZ))
MP_PEERS = sorted(
    [(b, c) for b in range(NX) for c in range(NC) if (b, c) != (0, 0)],
    key=lambda o: -ring(o[0], NX),
)


def split3(x):
    hi = x.astype(BF16)
    rest = x - hi.astype(F32)
    mid = rest.astype(BF16)
    low = (rest - mid.astype(F32)).astype(BF16)
    return hi, mid, low


def stack3(x):
    return jnp.concatenate(split3(x), axis=0)


def sum3(x):
    n = x.shape[0] // 3
    return x[:n] + (x[n : 2 * n] + x[2 * n :])


def dot(a, b, ca, cb):
    return lax.dot_general(a, b, (((ca,), (cb,)), ((), ())), preferred_element_type=F32)


def dot_high(a, b, ca, cb):
    return lax.dot_general(
        a, b, (((ca,), (cb,)), ((), ())), precision=HIGHEST, preferred_element_type=F32
    )


def chunk(index):
    row = pl.multiple_of((index // 8) * CB, CB)
    lane = pl.multiple_of(lax.rem(index, 8) * CL, CL)
    return pl.ds(row, CB), pl.ds(lane, CL)


def inverse_factors(gram):
    lane = lax.broadcasted_iota(jnp.int32, (R, 128), 1)
    row = lax.broadcasted_iota(jnp.int32, (R, 128), 0)
    first = lax.rem(lane // R, 2) == 0
    unit = jnp.where(lax.rem(lane, R) == row, 1.0, 0.0).astype(F32)
    w = jnp.where(lane < 2 * R, gram, unit)
    for k in range(R - 1):
        pivot_row = w[k : k + 1, :]
        f0 = w[:, k : k + 1] / pivot_row[:, k : k + 1]
        f1 = w[:, R + k : R + k + 1] / pivot_row[:, R + k : R + k + 1]
        factor = jnp.where(first, f0, f1)
        w = w - jnp.where(row > k, factor * pivot_row, 0.0)
    on0 = jnp.sum(jnp.where(lane == row, w, 0.0), axis=1, keepdims=True)
    on1 = jnp.sum(jnp.where(lane == row + R, w, 0.0), axis=1, keepdims=True)
    w = w * jnp.where(first, 1.0 / jnp.sqrt(on0), 1.0 / jnp.sqrt(on1))
    return w[:, 2 * R : 3 * R], w[:, 3 * R : 4 * R]


def exchange(
    a_hbm, g_hbm, f_hbm, qt_hbm, mat, phat, q_full, inv,
    a, g, f, qt, at, mhi, mlo, p_part, p_recv, p_full,
    gram_own, gram_recv, q_part, q_recv, z_recv,
    load_sem, send_sem, recv_sem,
):
    dp, mp = lax.axis_index("dp"), lax.axis_index("mp")
    y, z, x, c = dp // NZ, lax.rem(dp, NZ), mp // NC, lax.rem(mp, NC)
    block_id = y * 8 + mp

    def dp_target(o):
        return (lax.rem(y + o[0], NY) * NZ + lax.rem(z + o[1], NZ), mp)

    def block_target(o):
        return (
            lax.rem(y + o[0], NY) * NZ + z,
            lax.rem(x + o[1], NX) * NC + lax.rem(c + o[2], NC),
        )

    def z_target(o):
        return (y * NZ + lax.rem(z + o, NZ), mp)

    barrier = pltpu.get_barrier_semaphore()
    greeted = [dp_target(o) for o in DP_PEERS]
    greeted += [block_target(o) for o in BLOCK_PEERS if o[1:] != (0, 0)]
    for target in greeted:
        pl.semaphore_signal(barrier, inc=1, device_id=target, device_id_type=MESH)

    half = [pl.ds(m * KVW, KVW) for m in range(2)]
    loads = {}

    def load(name, src, dst):
        loads[name] = pltpu.make_async_copy(src, dst, load_sem.at[len(loads)])
        loads[name].start()

    load("q", qt_hbm, qt)
    load("g0", g_hbm.at[:, half[0]], g.at[pl.ds(0, TOK), half[0]])
    load("a", a_hbm, a.at[pl.ds(0, TOK), :])
    load("f0", f_hbm.at[:, half[0]], f.at[:, half[0]])
    load("g1", g_hbm.at[:, half[1]], g.at[pl.ds(0, TOK), half[1]])
    load("f1", f_hbm.at[:, half[1]], f.at[:, half[1]])
    g[TOK:, :] = jnp.zeros((TOK_PAD - TOK, WIDTH), BF16)
    a[TOK:, :] = jnp.zeros((TOK_PAD - TOK, ROWS), BF16)

    def send(src, dst, target, which):
        pltpu.make_async_remote_copy(
            src_ref=src,
            dst_ref=dst,
            send_sem=send_sem.at[which],
            recv_sem=recv_sem.at[which],
            device_id=target,
            device_id_type=MESH,
        ).start()

    def wait_on(sem, view):
        pltpu.make_async_copy(view, view, sem).wait()

    loads["q"].wait()
    for m in range(2):
        q3 = stack3(qt[pl.ds(m * R, R), :])
        loads[f"g{m}"].wait()
        inner3 = stack3(sum3(dot(q3, g[:, m * KVW : (m + 1) * KVW], 1, 1)))
        if m == 0:
            loads["a"].wait()
        part = sum3(dot(inner3, a[...], 1, 0))
        loads[f"f{m}"].wait()
        p_part[m] = part + sum3(dot(q3, f[:, m * KVW : (m + 1) * KVW], 1, 1))
        if m == 0:
            pl.semaphore_wait(barrier, len(greeted))
        for i, o in enumerate(DP_PEERS):
            target = dp_target(o)
            row, lane = chunk(target[0])
            send(p_part.at[m, row, lane], p_recv.at[m, i], target, m)

    at[...] = a[...].T

    def columns(n):
        lanes = pl.ds(pl.multiple_of(n * 256, 256), 256)
        block = dot(at[...], g[:, lanes], 1, 0) + f[:, lanes].astype(F32)
        mat[:, lanes] = block
        hi = block.astype(BF16)
        mhi[:, lanes] = hi
        mlo[:, lanes] = (block - hi.astype(F32)).astype(BF16)

    row, lane = chunk(dp)
    for m, first, last in ((0, 0, 4), (1, 4, 5)):
        pl.loop(first, last)(columns)
        wait_on(recv_sem.at[m], p_recv.at[m])
        own = p_part[m, row, lane]
        for i in range(N_PEERS):
            own = own + p_recv[m, i]
        p_full[m, row, lane] = own * (1.0 / 32)
        mine = p_full.at[m, row, lane]
        for o in DP_PEERS:
            send(mine, mine, dp_target(o), 2 + m)
    pl.loop(5, 8)(columns)

    for m in range(2):
        wait_on(recv_sem.at[2 + m], p_recv.at[m])
        cols = slice(m * KVW, (m + 1) * KVW)
        p3 = stack3(p_full[m])
        q_part[m] = sum3(dot(p3, mhi[:, cols], 1, 0) + dot(p3, mlo[:, cols], 1, 0))
        for i, o in enumerate(BLOCK_PEERS):
            target = block_target(o)
            r, l = chunk((target[0] // NZ) * 8 + target[1])
            send(q_part.at[m, r, l], q_recv.at[m, i], target, 4 + m)

    lane64 = lax.broadcasted_iota(jnp.int32, (R, 2 * R), 1)
    p_all = jnp.concatenate([p_full[0], p_full[1]], axis=0)
    both = dot_high(p_all, p_all, 1, 1)
    terms = jnp.where(lane64 < R, both[:R], both[R:])
    gram_own[...] = jnp.concatenate([terms, jnp.zeros((R, 128 - 2 * R), F32)], axis=1)
    for o in MP_PEERS:
        send(gram_own, gram_recv.at[mp], block_target((0,) + o), 10)
    gram_recv[mp] = gram_own[...]

    row, lane = chunk(block_id)
    for m in range(2):
        wait_on(recv_sem.at[4 + m], q_recv.at[m])
        own = q_part[m, row, lane]
        for i in range(N_PEERS):
            own = own + q_recv[m, i]
        z_recv[m, z] = own
        for o in Z_PEERS:
            send(z_recv.at[m, z], z_recv.at[m, z], z_target(o), 6 + m)

    wait_on(recv_sem.at[10], gram_recv.at[pl.ds(0, 7)])
    gram = gram_recv[0]
    for i in range(1, 8):
        gram = gram + gram_recv[i]
    inverses = inverse_factors(gram)

    for m in range(2):
        wait_on(recv_sem.at[6 + m], z_recv.at[m, pl.ds(0, 7)])
        own = z_recv[m, 0]
        for i in range(1, NZ):
            own = own + z_recv[m, i]
        q_full[m, row, lane] = own * (1.0 / 32)
        mine = q_full.at[m, row, lane]
        for o in BLOCK_PEERS:
            send(mine, mine, block_target(o), 8 + m)

    for m in range(2):
        inv[m] = inverses[m]
        hi, low, _ = split3(dot_high(inverses[m], p_full[m], 1, 0))
        phat[m] = jnp.concatenate([hi, low, hi, jnp.zeros_like(hi)], axis=0).T

    for m in range(2):
        wait_on(recv_sem.at[8 + m], q_recv.at[m])

    for m in range(2):
        wait_on(send_sem.at[m], p_recv.at[m])
        wait_on(send_sem.at[2 + m], p_recv.at[m])
        wait_on(send_sem.at[4 + m], q_recv.at[m])
        wait_on(send_sem.at[6 + m], z_recv.at[m, pl.ds(0, 7)])
        wait_on(send_sem.at[8 + m], q_recv.at[m])
    wait_on(send_sem.at[10], gram_recv.at[pl.ds(0, 7)])


def finish(mat, phat, q_full, inv, err_hbm, qn_hbm, err, qn, out_sem):
    laid = []
    for m in range(2):
        q_new = dot_high(inv[m], q_full[m], 1, 0)
        qn[pl.ds(m * R, R), :] = q_new
        hi, low, _ = split3(q_new)
        laid.append(jnp.concatenate([hi, hi, low, jnp.zeros_like(hi)], axis=0))
    outs = [pltpu.make_async_copy(qn, qn_hbm, out_sem.at[8])]
    outs[0].start()
    for i in range(8):
        rows = pl.ds(i * 128, 128)
        for m in range(2):
            cols = slice(m * KVW, (m + 1) * KVW)
            rebuilt = dot(phat[m, rows, :], laid[m], 1, 0)
            err[rows, cols] = (mat[rows, cols] - rebuilt).astype(BF16)
        copy = pltpu.make_async_copy(err.at[rows, :], err_hbm.at[rows, :], out_sem.at[i])
        copy.start()
        outs.append(copy)
    for copy in outs:
        copy.wait()


def per_device(activations, out_grads, feedback, q_prev):
    qt = jnp.transpose(q_prev, (1, 2, 0)).reshape(2 * R, KVW)
    any_space = pl.BlockSpec(memory_space=pl.ANY)
    vmem = pl.BlockSpec(memory_space=pltpu.VMEM)
    held = pl.pallas_call(
        exchange,
        out_shape=(
            pltpu.VMEM((ROWS, WIDTH), F32),
            pltpu.VMEM((2, ROWS, 128), BF16),
            pltpu.VMEM((2, R, KVW), F32),
            pltpu.VMEM((2, R, R), F32),
        ),
        in_specs=[any_space] * 4,
        out_specs=(vmem,) * 4,
        scratch_shapes=[
            pltpu.VMEM((TOK_PAD, ROWS), BF16),
            pltpu.VMEM((TOK_PAD, WIDTH), BF16),
            pltpu.VMEM((ROWS, WIDTH), BF16),
            pltpu.VMEM((2 * R, KVW), F32),
            pltpu.VMEM((ROWS, TOK_PAD), BF16),
            pltpu.VMEM((ROWS, WIDTH), BF16),
            pltpu.VMEM((ROWS, WIDTH), BF16),
            pltpu.VMEM((2, R, ROWS), F32),
            pltpu.VMEM((2, N_PEERS, CB, CL), F32),
            pltpu.VMEM((2, R, ROWS), F32),
            pltpu.VMEM((R, 128), F32),
            pltpu.VMEM((8, R, 128), F32),
            pltpu.VMEM((2, R, KVW), F32),
            pltpu.VMEM((2, N_PEERS, CB, CL), F32),
            pltpu.VMEM((2, NZ, CB, CL), F32),
            pltpu.SemaphoreType.DMA((6,)),
            pltpu.SemaphoreType.DMA((11,)),
            pltpu.SemaphoreType.DMA((11,)),
        ],
        compiler_params=pltpu.CompilerParams(
            collective_id=0, has_side_effects=True, vmem_limit_bytes=40 * 2**20
        ),
    )(*[pltpu.with_memory_space_constraint(v, pltpu.HBM) for v in (activations, out_grads, feedback[0], qt)])
    err, qn = pl.pallas_call(
        finish,
        out_shape=(
            jax.ShapeDtypeStruct((ROWS, WIDTH), BF16),
            jax.ShapeDtypeStruct((2 * R, KVW), F32),
        ),
        in_specs=[vmem] * 4,
        out_specs=(any_space,) * 2,
        scratch_shapes=[
            pltpu.VMEM((ROWS, WIDTH), BF16),
            pltpu.VMEM((2 * R, KVW), F32),
            pltpu.SemaphoreType.DMA((9,)),
        ],
        compiler_params=pltpu.CompilerParams(vmem_limit_bytes=24 * 2**20),
    )(*held)
    q_new = jnp.transpose(qn.reshape(2, R, KVW), (2, 0, 1))
    return err[None], q_new


def solution(mesh):
    return jax.shard_map(
        per_device,
        mesh=mesh,
        in_specs=(P("dp", "mp"), P("dp", None), P("dp", "mp", None), P()),
        out_specs=(P("dp", "mp", None), P()),
        check_vma=False,
    )
```

time: 57.8 us -> 47.1 us (0.81)
  local copies, waits for them, and re-layouts: 5.54 us -> 0 us
  Pallas kernels: 51.5 us -> 46.4 us
    unnamed x4 -> x0, local copies, waits for them, and re-layouts: 5.54 us -> none
    pallas_call x1 -> x2, Pallas kernels: 51.5 us -> 46.4 us  [the longest x1 43.8 us: per_device(): pl.pallas_call(exchange, out_shape=(pltpu.VMEM((ROWS, WIDTH), F32), pltpu...]
where the time goes in v2:
time: 47.1 us; the launch traced here: 47 us
  Pallas kernels  46.4 us (99%)
  between operations  0.64 us (1%)
    pallas_call x1, Pallas kernels, per_device(): pl.pallas_call(exchange, out_shape=(pltpu.VMEM((ROWS, WIDTH), F32), pltpu...  43.8 us
    pallas_call x1, Pallas kernels, per_device(): pl.pallas_call(finish, out_shape=(jax.ShapeDtypeStruct((ROWS, WIDTH), BF1...  2.62 us

profile of v2, /device:TPU:1, one launch (start us, length us, event | category | flops | bytes accessed | tf_op | source)
XLA Modules:
  0.0 47.0 jit_solution(584768370167670589)
XLA Ops:
  0.6 43.8 %shard_map.59 = (f32[1024,2048]{1,0:T(8,128)S(1)}, bf16[2,1024,128]{2,1,0:T(8,128)(2,1)S(1)}, f32[2,32,1024]{2,1,0:T(8,128)S(1)}, f32[2,32,32]{2,1,0:T(8,128)S(1)}) custom-call(bf16[1440,1024]{1,0:T(8,128)(2,1)} %a_hbm.1, bf16[1440,2048]{1,0:T(8,128)(2,1)} %g_hbm.1, bf16[1024,2048]{1,0:T(8,128)(2,1)} %bitcast.8, f32[64,1024]{1,0:T(8,128)} %bitcast.9), custom_call_target="tpu_custom_call" | custom-call | tf_op jit(solution)/shard_map/pallas_call | solution.py:279
  44.4 2.6 %shard_map.60 = (bf16[1024,2048]{1,0:T(8,128)(2,1)}, f32[64,1024]{1,0:T(8,128)}) custom-call(f32[1024,2048]{1,0:T(8,128)S(1)} %get-tuple-element.8.mat, bf16[2,1024,128]{2,1,0:T(8,128)(2,1)S(1)} %get-tuple-element.9.phat, f32[2,32,1024]{2,1,0:T(8,128)S(1)} %get-tuple-element.10.q_full, f32[2,32,32]{2,1,0:T(8,128)S(1)} %get-tuple-element.11.inv), custom_call_target="tpu_custom_call" | custom-call | tf_op jit(solution)/shard_map/pallas_call | solution.py:313

commit v3 on v2

--- a/solution.py
+++ b/solution.py
@@ -33,6 +33,7 @@
     [(a, b, c) for a in range(NY) for b in range(NX) for c in range(NC) if (a, b, c) != (0, 0, 0)],
     key=lambda o: -(ring(o[0], NY) + ring(o[1], NX)),
 )
+FAR_Y = (2, 1, 3, 0)
 Z_PEERS = sorted(range(1, NZ), key=lambda o: -ring(o, NZ))
 MP_PEERS = sorted(
     [(b, c) for b in range(NX) for c in range(NC) if (b, c) != (0, 0)],
@@ -50,6 +51,15 @@
 
 def stack3(x):
     return jnp.concatenate(split3(x), axis=0)
+
+
+def lay(x, order):
+    parts = split3(x)
+    return jnp.concatenate([parts[i] for i in order] + [jnp.zeros_like(parts[0])] * 2, axis=0)
+
+
+LEFT_PARTS = (0, 0, 1, 1, 0, 2)
+RIGHT_PARTS = (0, 1, 0, 1, 2, 0)
 
 
 def sum3(x):
@@ -92,8 +102,8 @@
 
 
 def exchange(
-    a_hbm, g_hbm, f_hbm, qt_hbm, mat, phat, q_full, inv,
-    a, g, f, qt, at, mhi, mlo, p_part, p_recv, p_full,
+    a_hbm, g_hbm, f_hbm, qt_hbm, err0, qn0, mat1, left1, q_full, inv1,
+    a, g, f, qt, at, mat0, left0, mhi, mlo, p_part, p_recv, p_full,
     gram_own, gram_recv, q_part, q_recv, z_recv,
     load_sem, send_sem, recv_sem,
 ):
@@ -127,20 +137,24 @@
         loads[name].start()
 
     load("q", qt_hbm, qt)
-    load("g0", g_hbm.at[:, half[0]], g.at[pl.ds(0, TOK), half[0]])
-    load("a", a_hbm, a.at[pl.ds(0, TOK), :])
-    load("f0", f_hbm.at[:, half[0]], f.at[:, half[0]])
-    load("g1", g_hbm.at[:, half[1]], g.at[pl.ds(0, TOK), half[1]])
-    load("f1", f_hbm.at[:, half[1]], f.at[:, half[1]])
+    for m in range(2):
+        load(f"g{m}", g_hbm.at[:, half[m]], g.at[pl.ds(0, TOK), half[m]])
+        if m == 0:
+            load("a", a_hbm, a.at[pl.ds(0, TOK), :])
+        load(f"f{m}", f_hbm.at[:, half[m]], f.at[:, half[m]])
     g[TOK:, :] = jnp.zeros((TOK_PAD - TOK, WIDTH), BF16)
     a[TOK:, :] = jnp.zeros((TOK_PAD - TOK, ROWS), BF16)
 
-    def send(src, dst, target, which):
+    def arrival(dz, m):
+        opposite = lax.rem(lax.rem(z + dz, NZ) // 2 + 2, 4) == z // 2
+        return jnp.where(opposite, 11 + m, 2 + m)
+
+    def send(src, dst, target, which, arrives=None):
         pltpu.make_async_remote_copy(
             src_ref=src,
             dst_ref=dst,
             send_sem=send_sem.at[which],
-            recv_sem=recv_sem.at[which],
+            recv_sem=recv_sem.at[which if arrives is None else arrives],
             device_id=target,
             device_id_type=MESH,
         ).start()
@@ -150,16 +164,17 @@
 
     loads["q"].wait()
     for m in range(2):
+        cols = slice(m * KVW, (m + 1) * KVW)
         q3 = stack3(qt[pl.ds(m * R, R), :])
         loads[f"g{m}"].wait()
-        inner3 = stack3(sum3(dot(q3, g[:, m * KVW : (m + 1) * KVW], 1, 1)))
+        inner3 = stack3(sum3(dot(q3, g[:, cols], 1, 1)))
         if m == 0:
             loads["a"].wait()
-        part = sum3(dot(inner3, a[...], 1, 0))
         loads[f"f{m}"].wait()
-        p_part[m] = part + sum3(dot(q3, f[:, m * KVW : (m + 1) * KVW], 1, 1))
         if m == 0:
             pl.semaphore_wait(barrier, len(greeted))
+        part = sum3(dot(inner3, a[...], 1, 0))
+        p_part[m] = part + sum3(dot(q3, f[:, cols], 1, 1))
         for i, o in enumerate(DP_PEERS):
             target = dp_target(o)
             row, lane = chunk(target[0])
@@ -168,16 +183,16 @@
     at[...] = a[...].T
 
     def columns(n):
-        lanes = pl.ds(pl.multiple_of(n * 256, 256), 256)
+        m, lanes = n // 2, slice(n * 512, (n + 1) * 512)
         block = dot(at[...], g[:, lanes], 1, 0) + f[:, lanes].astype(F32)
-        mat[:, lanes] = block
+        (mat0, mat1)[m][:, (n % 2) * 512 : (n % 2 + 1) * 512] = block
         hi = block.astype(BF16)
         mhi[:, lanes] = hi
         mlo[:, lanes] = (block - hi.astype(F32)).astype(BF16)
 
     row, lane = chunk(dp)
-    for m, first, last in ((0, 0, 4), (1, 4, 5)):
-        pl.loop(first, last)(columns)
+    for m in range(2):
+        columns(m)
         wait_on(recv_sem.at[m], p_recv.at[m])
         own = p_part[m, row, lane]
         for i in range(N_PEERS):
@@ -185,14 +200,23 @@
         p_full[m, row, lane] = own * (1.0 / 32)
         mine = p_full.at[m, row, lane]
         for o in DP_PEERS:
-            send(mine, mine, dp_target(o), 2 + m)
-    pl.loop(5, 8)(columns)
-
-    for m in range(2):
-        wait_on(recv_sem.at[2 + m], p_recv.at[m])
-        cols = slice(m * KVW, (m + 1) * KVW)
-        p3 = stack3(p_full[m])
-        q_part[m] = sum3(dot(p3, mhi[:, cols], 1, 0) + dot(p3, mlo[:, cols], 1, 0))
+            send(mine, mine, dp_target(o), 2 + m, arrival(o[1], m))
+    columns(2)
+    columns(3)
+
+    for m in range(2):
+        terms = []
+        for step in (1, 3, 0, 2):
+            if step == 1:
+                wait_on(recv_sem.at[2 + m], p_recv.at[m, pl.ds(0, N_PEERS - 8)])
+            if step == 2:
+                wait_on(recv_sem.at[11 + m], p_recv.at[m, pl.ds(0, 8)])
+            pair = lax.rem(z // 2 + step, 4)
+            wide = pl.ds(pl.multiple_of(pair * 256, 256), 256)
+            cols = slice(m * KVW, (m + 1) * KVW)
+            p3 = stack3(p_full[m, :, wide])
+            terms.append(dot(p3, mhi[wide, cols], 1, 0) + dot(p3, mlo[wide, cols], 1, 0))
+        q_part[m] = sum3(terms[0] + terms[1] + terms[2] + terms[3])
         for i, o in enumerate(BLOCK_PEERS):
             target = block_target(o)
             r, l = chunk((target[0] // NZ) * 8 + target[1])
@@ -233,13 +257,20 @@
         for o in BLOCK_PEERS:
             send(mine, mine, block_target(o), 8 + m)
 
-    for m in range(2):
-        inv[m] = inverses[m]
-        hi, low, _ = split3(dot_high(inverses[m], p_full[m], 1, 0))
-        phat[m] = jnp.concatenate([hi, low, hi, jnp.zeros_like(hi)], axis=0).T
-
-    for m in range(2):
-        wait_on(recv_sem.at[8 + m], q_recv.at[m])
+    inv1[...] = inverses[1]
+    for m in range(2):
+        normed = dot_high(inverses[m], p_full[m], 1, 0)
+        left = dot_high(inverses[m], normed, 0, 0)
+        (left0, left1)[m][...] = lay(left, LEFT_PARTS).T
+
+    wait_on(recv_sem.at[8], q_recv.at[0])
+    raw = q_full[0]
+    laid = lay(raw, RIGHT_PARTS)
+    for i in range(4):
+        rows = pl.ds(i * 256, 256)
+        err0[rows, :] = (mat0[rows, :] - dot(left0[rows, :], laid, 1, 0)).astype(BF16)
+    qn0[...] = dot_high(inverses[0], raw, 1, 0)
+    wait_on(recv_sem.at[9], q_recv.at[1])
 
     for m in range(2):
         wait_on(send_sem.at[m], p_recv.at[m])
@@ -250,24 +281,23 @@
     wait_on(send_sem.at[10], gram_recv.at[pl.ds(0, 7)])
 
 
-def finish(mat, phat, q_full, inv, err_hbm, qn_hbm, err, qn, out_sem):
-    laid = []
-    for m in range(2):
-        q_new = dot_high(inv[m], q_full[m], 1, 0)
-        qn[pl.ds(m * R, R), :] = q_new
-        hi, low, _ = split3(q_new)
-        laid.append(jnp.concatenate([hi, hi, low, jnp.zeros_like(hi)], axis=0))
-    outs = [pltpu.make_async_copy(qn, qn_hbm, out_sem.at[8])]
-    outs[0].start()
-    for i in range(8):
-        rows = pl.ds(i * 128, 128)
-        for m in range(2):
-            cols = slice(m * KVW, (m + 1) * KVW)
-            rebuilt = dot(phat[m, rows, :], laid[m], 1, 0)
-            err[rows, cols] = (mat[rows, cols] - rebuilt).astype(BF16)
-        copy = pltpu.make_async_copy(err.at[rows, :], err_hbm.at[rows, :], out_sem.at[i])
-        copy.start()
-        outs.append(copy)
+def finish(err0, qn0, mat1, left1, q_full, inv1, err_hbm, qn_hbm, err1, qn1, out_sem):
+    outs = []
+
+    def store(src, dst):
+        outs.append(pltpu.make_async_copy(src, dst, out_sem.at[len(outs)]))
+        outs[-1].start()
+
+    store(err0, err_hbm.at[:, pl.ds(0, KVW)])
+    store(qn0, qn_hbm.at[pl.ds(0, R), :])
+    raw = q_full[1]
+    laid = lay(raw, RIGHT_PARTS)
+    for i in range(4):
+        rows = pl.ds(i * 256, 256)
+        err1[rows, :] = (mat1[rows, :] - dot(left1[rows, :], laid, 1, 0)).astype(BF16)
+        store(err1.at[rows, :], err_hbm.at[rows, pl.ds(KVW, KVW)])
+    qn1[...] = dot_high(inv1[...], raw, 1, 0)
+    store(qn1, qn_hbm.at[pl.ds(R, R), :])
     for copy in outs:
         copy.wait()
 
@@ -279,19 +309,23 @@
     held = pl.pallas_call(
         exchange,
         out_shape=(
-            pltpu.VMEM((ROWS, WIDTH), F32),
-            pltpu.VMEM((2, ROWS, 128), BF16),
+            pltpu.VMEM((ROWS, KVW), BF16),
+            pltpu.VMEM((R, KVW), F32),
+            pltpu.VMEM((ROWS, KVW), F32),
+            pltpu.VMEM((ROWS, 256), BF16),
             pltpu.VMEM((2, R, KVW), F32),
-            pltpu.VMEM((2, R, R), F32),
+            pltpu.VMEM((R, R), F32),
         ),
         in_specs=[any_space] * 4,
-        out_specs=(vmem,) * 4,
+        out_specs=(vmem,) * 6,
         scratch_shapes=[
             pltpu.VMEM((TOK_PAD, ROWS), BF16),
             pltpu.VMEM((TOK_PAD, WIDTH), BF16),
             pltpu.VMEM((ROWS, WIDTH), BF16),
             pltpu.VMEM((2 * R, KVW), F32),
             pltpu.VMEM((ROWS, TOK_PAD), BF16),
+            pltpu.VMEM((ROWS, KVW), F32),
+            pltpu.VMEM((ROWS, 256), BF16),
             pltpu.VMEM((ROWS, WIDTH), BF16),
             pltpu.VMEM((ROWS, WIDTH), BF16),
             pltpu.VMEM((2, R, ROWS), F32),
@@ -302,9 +336,9 @@
             pltpu.VMEM((2, R, KVW), F32),
             pltpu.VMEM((2, N_PEERS, CB, CL), F32),
             pltpu.VMEM((2, NZ, CB, CL), F32),
-            pltpu.SemaphoreType.DMA((6,)),
+            pltpu.SemaphoreType.DMA((10,)),
             pltpu.SemaphoreType.DMA((11,)),
-            pltpu.SemaphoreType.DMA((11,)),
+            pltpu.SemaphoreType.DMA((13,)),
         ],
         compiler_params=pltpu.CompilerParams(
             collective_id=0, has_side_effects=True, vmem_limit_bytes=40 * 2**20
@@ -316,12 +350,12 @@
             jax.ShapeDtypeStruct((ROWS, WIDTH), BF16),
             jax.ShapeDtypeStruct((2 * R, KVW), F32),
         ),
-        in_specs=[vmem] * 4,
+        in_specs=[vmem] * 6,
         out_specs=(any_space,) * 2,
         scratch_shapes=[
-            pltpu.VMEM((ROWS, WIDTH), BF16),
-            pltpu.VMEM((2 * R, KVW), F32),
-            pltpu.SemaphoreType.DMA((9,)),
+            pltpu.VMEM((ROWS, KVW), BF16),
+            pltpu.VMEM((R, KVW), F32),
+            pltpu.SemaphoreType.DMA((7,)),
         ],
         compiler_params=pltpu.CompilerParams(vmem_limit_bytes=24 * 2**20),
     )(*held)

time: 47.1 us -> 45.8 us (0.972)
  Pallas kernels: 46.4 us -> 45.1 us
    pallas_call x1, Pallas kernels: 43.8 us -> 42.9 us  [per_device(): pl.pallas_call(exchange, out_shape=(pltpu.VMEM((ROWS, KVW), BF16), pltpu....]
    pallas_call x1, Pallas kernels: 2.62 us -> 2.14 us  [per_device(): pl.pallas_call(finish, out_shape=(jax.ShapeDtypeStruct((ROWS, WIDTH), BF1...]
where the time goes in v3:
time: 45.8 us; the launch traced here: 45.7 us
  Pallas kernels  45.1 us (98%)
  between operations  0.64 us (1%)
    pallas_call x1, Pallas kernels, per_device(): pl.pallas_call(exchange, out_shape=(pltpu.VMEM((ROWS, KVW), BF16), pltpu....  42.9 us
    pallas_call x1, Pallas kernels, per_device(): pl.pallas_call(finish, out_shape=(jax.ShapeDtypeStruct((ROWS, WIDTH), BF1...  2.14 us

profile of v3, /device:TPU:1, one launch (start us, length us, event | category | flops | bytes accessed | tf_op | source)
XLA Modules:
  0.0 45.7 jit_solution(9328090633687337729)
XLA Ops:
  0.6 42.9 %shard_map.59 = (bf16[1024,1024]{1,0:T(8,128)(2,1)S(1)}, f32[32,1024]{1,0:T(8,128)S(1)}, f32[1024,1024]{1,0:T(8,128)S(1)}, bf16[1024,256]{1,0:T(8,128)(2,1)S(1)}...) custom-call(bf16[1440,1024]{1,0:T(8,128)(2,1)} %a_hbm.1, bf16[1440,2048]{1,0:T(8,128)(2,1)} %g_hbm.1, ...), custom_call_target="tpu_custom_call" | custom-call | tf_op jit(solution)/shard_map/pallas_call | solution.py:309
  43.6 2.1 %shard_map.60 = (bf16[1024,2048]{1,0:T(8,128)(2,1)}, f32[64,1024]{1,0:T(8,128)}) custom-call(bf16[1024,1024]{1,0:T(8,128)(2,1)S(1)} %get-tuple-element.10.err0, f32[32,1024]{1,0:T(8,128)S(1)} %get-tuple-element.11.qn0, f32[1024,1024]{1,0:T(8,128)S(1)} %get-tuple-element.12.mat1, bf16[1024,256]{1,0:T(8,128)(2,1)S(1)} %get-tuple-element.13.left1, ...), custom_call_target="tpu_custom_call" | custom-call | tf_op jit(solution)/shard_map/pallas_call | solution.py:347

commit v4 on v3

--- a/solution.py
+++ b/solution.py
@@ -60,6 +60,7 @@
 
 LEFT_PARTS = (0, 0, 1, 1, 0, 2)
 RIGHT_PARTS = (0, 1, 0, 1, 2, 0)
+ERR0_CUTS = 4
 
 
 def sum3(x):
@@ -102,7 +103,7 @@
 
 
 def exchange(
-    a_hbm, g_hbm, f_hbm, qt_hbm, err0, qn0, mat1, left1, q_full, inv1,
+    a_hbm, g_hbm, f_hbm, qt_hbm, err0, mat1, left1, q_full, inv,
     a, g, f, qt, at, mat0, left0, mhi, mlo, p_part, p_recv, p_full,
     gram_own, gram_recv, q_part, q_recv, z_recv,
     load_sem, send_sem, recv_sem,
@@ -123,25 +124,25 @@
     def z_target(o):
         return (y * NZ + lax.rem(z + o, NZ), mp)
 
+    half = [pl.ds(m * KVW, KVW) for m in range(2)]
+    loads = {}
+
+    def load(name, src, dst):
+        loads[name] = pltpu.make_async_copy(src, dst, load_sem.at[len(loads)])
+        loads[name].start()
+
+    load("q", qt_hbm, qt)
+    for m in range(2):
+        load(f"g{m}", g_hbm.at[:, half[m]], g.at[pl.ds(0, TOK), half[m]])
+        if m == 0:
+            load("a", a_hbm, a.at[pl.ds(0, TOK), :])
+        load(f"f{m}", f_hbm.at[:, half[m]], f.at[:, half[m]])
     barrier = pltpu.get_barrier_semaphore()
     greeted = [dp_target(o) for o in DP_PEERS]
     greeted += [block_target(o) for o in BLOCK_PEERS if o[1:] != (0, 0)]
     for target in greeted:
         pl.semaphore_signal(barrier, inc=1, device_id=target, device_id_type=MESH)
 
-    half = [pl.ds(m * KVW, KVW) for m in range(2)]
-    loads = {}
-
-    def load(name, src, dst):
-        loads[name] = pltpu.make_async_copy(src, dst, load_sem.at[len(loads)])
-        loads[name].start()
-
-    load("q", qt_hbm, qt)
-    for m in range(2):
-        load(f"g{m}", g_hbm.at[:, half[m]], g.at[pl.ds(0, TOK), half[m]])
-        if m == 0:
-            load("a", a_hbm, a.at[pl.ds(0, TOK), :])
-        load(f"f{m}", f_hbm.at[:, half[m]], f.at[:, half[m]])
     g[TOK:, :] = jnp.zeros((TOK_PAD - TOK, WIDTH), BF16)
     a[TOK:, :] = jnp.zeros((TOK_PAD - TOK, ROWS), BF16)
 
@@ -162,19 +163,22 @@
     def wait_on(sem, view):
         pltpu.make_async_copy(view, view, sem).wait()
 
-    loads["q"].wait()
-    for m in range(2):
+    def left_factors(m):
         cols = slice(m * KVW, (m + 1) * KVW)
         q3 = stack3(qt[pl.ds(m * R, R), :])
         loads[f"g{m}"].wait()
         inner3 = stack3(sum3(dot(q3, g[:, cols], 1, 1)))
         if m == 0:
             loads["a"].wait()
+        part = sum3(dot(inner3, a[...], 1, 0))
         loads[f"f{m}"].wait()
+        p_part[m] = part + sum3(dot(q3, f[:, cols], 1, 1))
+
+    loads["q"].wait()
+    for m in range(2):
+        pl.when(dp >= 0)(functools.partial(left_factors, m))
         if m == 0:
             pl.semaphore_wait(barrier, len(greeted))
-        part = sum3(dot(inner3, a[...], 1, 0))
-        p_part[m] = part + sum3(dot(q3, f[:, cols], 1, 1))
         for i, o in enumerate(DP_PEERS):
             target = dp_target(o)
             row, lane = chunk(target[0])
@@ -257,7 +261,15 @@
         for o in BLOCK_PEERS:
             send(mine, mine, block_target(o), 8 + m)
 
-    inv1[...] = inverses[1]
+    for m in range(2):
+        wait_on(send_sem.at[m], p_recv.at[m])
+        wait_on(send_sem.at[2 + m], p_recv.at[m])
+        wait_on(send_sem.at[4 + m], q_recv.at[m])
+        wait_on(send_sem.at[6 + m], z_recv.at[m, pl.ds(0, 7)])
+    wait_on(send_sem.at[10], gram_recv.at[pl.ds(0, 7)])
+
+    inv[0] = inverses[0]
+    inv[1] = inverses[1]
     for m in range(2):
         normed = dot_high(inverses[m], p_full[m], 1, 0)
         left = dot_high(inverses[m], normed, 0, 0)
@@ -269,35 +281,30 @@
     for i in range(4):
         rows = pl.ds(i * 256, 256)
         err0[rows, :] = (mat0[rows, :] - dot(left0[rows, :], laid, 1, 0)).astype(BF16)
-    qn0[...] = dot_high(inverses[0], raw, 1, 0)
     wait_on(recv_sem.at[9], q_recv.at[1])
 
     for m in range(2):
-        wait_on(send_sem.at[m], p_recv.at[m])
-        wait_on(send_sem.at[2 + m], p_recv.at[m])
-        wait_on(send_sem.at[4 + m], q_recv.at[m])
-        wait_on(send_sem.at[6 + m], z_recv.at[m, pl.ds(0, 7)])
         wait_on(send_sem.at[8 + m], q_recv.at[m])
-    wait_on(send_sem.at[10], gram_recv.at[pl.ds(0, 7)])
-
-
-def finish(err0, qn0, mat1, left1, q_full, inv1, err_hbm, qn_hbm, err1, qn1, out_sem):
+
+
+def finish(err0, mat1, left1, q_full, inv, err_hbm, qn_hbm, err1, qn, out_sem):
     outs = []
 
     def store(src, dst):
         outs.append(pltpu.make_async_copy(src, dst, out_sem.at[len(outs)]))
         outs[-1].start()
 
-    store(err0, err_hbm.at[:, pl.ds(0, KVW)])
-    store(qn0, qn_hbm.at[pl.ds(0, R), :])
-    raw = q_full[1]
-    laid = lay(raw, RIGHT_PARTS)
+    for i in range(ERR0_CUTS):
+        rows = pl.ds(i * (ROWS // ERR0_CUTS), ROWS // ERR0_CUTS)
+        store(err0.at[rows, :], err_hbm.at[rows, pl.ds(0, KVW)])
+    laid = lay(q_full[1], RIGHT_PARTS)
     for i in range(4):
         rows = pl.ds(i * 256, 256)
         err1[rows, :] = (mat1[rows, :] - dot(left1[rows, :], laid, 1, 0)).astype(BF16)
         store(err1.at[rows, :], err_hbm.at[rows, pl.ds(KVW, KVW)])
-    qn1[...] = dot_high(inv1[...], raw, 1, 0)
-    store(qn1, qn_hbm.at[pl.ds(R, R), :])
+    for m in range(2):
+        qn[pl.ds(m * R, R), :] = dot_high(inv[m], q_full[m], 1, 0)
+    store(qn, qn_hbm)
     for copy in outs:
         copy.wait()
 
@@ -310,14 +317,13 @@
         exchange,
         out_shape=(
             pltpu.VMEM((ROWS, KVW), BF16),
-            pltpu.VMEM((R, KVW), F32),
             pltpu.VMEM((ROWS, KVW), F32),
             pltpu.VMEM((ROWS, 256), BF16),
             pltpu.VMEM((2, R, KVW), F32),
-            pltpu.VMEM((R, R), F32),
+            pltpu.VMEM((2, R, R), F32),
         ),
         in_specs=[any_space] * 4,
-        out_specs=(vmem,) * 6,
+        out_specs=(vmem,) * 5,
         scratch_shapes=[
             pltpu.VMEM((TOK_PAD, ROWS), BF16),
             pltpu.VMEM((TOK_PAD, WIDTH), BF16),
@@ -350,12 +356,12 @@
             jax.ShapeDtypeStruct((ROWS, WIDTH), BF16),
             jax.ShapeDtypeStruct((2 * R, KVW), F32),
         ),
-        in_specs=[vmem] * 6,
+        in_specs=[vmem] * 5,
         out_specs=(any_space,) * 2,
         scratch_shapes=[
             pltpu.VMEM((ROWS, KVW), BF16),
-            pltpu.VMEM((R, KVW), F32),
-            pltpu.SemaphoreType.DMA((7,)),
+            pltpu.VMEM((2 * R, KVW), F32),
+            pltpu.SemaphoreType.DMA((ERR0_CUTS + 5,)),
         ],
         compiler_params=pltpu.CompilerParams(vmem_limit_bytes=24 * 2**20),
     )(*held)

time: 45.8 us -> 44.9 us (0.980)
  Pallas kernels: 45.1 us -> 44 us
    pallas_call x1, Pallas kernels: 42.9 us -> 41.8 us  [per_device(): pl.pallas_call(exchange, out_shape=(pltpu.VMEM((ROWS, KVW), BF16), pltpu....]
where the time goes in v4:
time: 44.9 us; the launch traced here: 44.8 us
  Pallas kernels  44 us (98%)
  between operations  0.8 us (2%)
    pallas_call x1, Pallas kernels, per_device(): pl.pallas_call(exchange, out_shape=(pltpu.VMEM((ROWS, KVW), BF16), pltpu....  41.8 us
    pallas_call x1, Pallas kernels, per_device(): pl.pallas_call(finish, out_shape=(jax.ShapeDtypeStruct((ROWS, WIDTH), BF1...  2.17 us

profile of v4, /device:TPU:1, one launch (start us, length us, event | category | flops | bytes accessed | tf_op | source)
XLA Modules:
  0.0 44.8 jit_solution(7881582452767794585)
XLA Ops:
  0.6 41.8 %shard_map.59 = (bf16[1024,1024]{1,0:T(8,128)(2,1)S(1)}, f32[1024,1024]{1,0:T(8,128)S(1)}, bf16[1024,256]{1,0:T(8,128)(2,1)S(1)}, f32[2,32,1024]{2,1,0:T(8,128)S(1)}, f32[2,32,32]{2,1,0:T(8,128)S(1)}) custom-call(bf16[1440,1024]{1,0:T(8,128)(2,1)} %a_hbm.1, bf16[1440,2048]{1,0:T(8,128)(2,1)} %g_hbm.1, bf16[1024,2048]{1,0:T(8,128)(2,1)} %bitcast.8, ...), custom_call_target="tpu_custom_call" | custom-call | tf_op jit(solution)/shard_map/pallas_call | solution.py:316
  42.5 2.2 %shard_map.60 = (bf16[1024,2048]{1,0:T(8,128)(2,1)}, f32[64,1024]{1,0:T(8,128)}) custom-call(bf16[1024,1024]{1,0:T(8,128)(2,1)S(1)} %get-tuple-element.9.err0, f32[1024,1024]{1,0:T(8,128)S(1)} %get-tuple-element.10.mat1, bf16[1024,256]{1,0:T(8,128)(2,1)S(1)} %get-tuple-element.11.left1, f32[2,32,1024]{2,1,0:T(8,128)S(1)} %get-tuple-element.12.q_full, ...), custom_call_target="tpu_custom_call" | custom-call | tf_op jit(solution)/shard_map/pallas_call | solution.py:353

commit v5 on v4

--- a/solution.py
+++ b/solution.py
@@ -60,7 +60,7 @@
 
 LEFT_PARTS = (0, 0, 1, 1, 0, 2)
 RIGHT_PARTS = (0, 1, 0, 1, 2, 0)
-ERR0_CUTS = 4
+ERR0_CUTS = 2
 
 
 def sum3(x):
@@ -134,9 +134,9 @@
     load("q", qt_hbm, qt)
     for m in range(2):
         load(f"g{m}", g_hbm.at[:, half[m]], g.at[pl.ds(0, TOK), half[m]])
+        load(f"f{m}", f_hbm.at[:, half[m]], f.at[:, half[m]])
         if m == 0:
             load("a", a_hbm, a.at[pl.ds(0, TOK), :])
-        load(f"f{m}", f_hbm.at[:, half[m]], f.at[:, half[m]])
     barrier = pltpu.get_barrier_semaphore()
     greeted = [dp_target(o) for o in DP_PEERS]
     greeted += [block_target(o) for o in BLOCK_PEERS if o[1:] != (0, 0)]
@@ -168,11 +168,11 @@
         q3 = stack3(qt[pl.ds(m * R, R), :])
         loads[f"g{m}"].wait()
         inner3 = stack3(sum3(dot(q3, g[:, cols], 1, 1)))
+        loads[f"f{m}"].wait()
+        part = sum3(dot(q3, f[:, cols], 1, 1))
         if m == 0:
             loads["a"].wait()
-        part = sum3(dot(inner3, a[...], 1, 0))
-        loads[f"f{m}"].wait()
-        p_part[m] = part + sum3(dot(q3, f[:, cols], 1, 1))
+        p_part[m] = part + sum3(dot(inner3, a[...], 1, 0))
 
     loads["q"].wait()
     for m in range(2):
@@ -298,8 +298,8 @@
         rows = pl.ds(i * (ROWS // ERR0_CUTS), ROWS // ERR0_CUTS)
         store(err0.at[rows, :], err_hbm.at[rows, pl.ds(0, KVW)])
     laid = lay(q_full[1], RIGHT_PARTS)
-    for i in range(4):
-        rows = pl.ds(i * 256, 256)
+    for i in range(8):
+        rows = pl.ds(i * 128, 128)
         err1[rows, :] = (mat1[rows, :] - dot(left1[rows, :], laid, 1, 0)).astype(BF16)
         store(err1.at[rows, :], err_hbm.at[rows, pl.ds(KVW, KVW)])
     for m in range(2):
@@ -361,7 +361,7 @@
         scratch_shapes=[
             pltpu.VMEM((ROWS, KVW), BF16),
             pltpu.VMEM((2 * R, KVW), F32),
-            pltpu.SemaphoreType.DMA((ERR0_CUTS + 5,)),
+            pltpu.SemaphoreType.DMA((ERR0_CUTS + 9,)),
         ],
         compiler_params=pltpu.CompilerParams(vmem_limit_bytes=24 * 2**20),
     )(*held)

time: 44.9 us -> 44.7 us (level)
  no operation moved by 1% of the time
where the time goes in v5:
time: 44.7 us; the launch traced here: 44.6 us
  Pallas kernels  43.8 us (98%)
  between operations  0.8 us (2%)
    pallas_call x1, Pallas kernels, per_device(): pl.pallas_call(exchange, out_shape=(pltpu.VMEM((ROWS, KVW), BF16), pltpu....  41.7 us
    pallas_call x1, Pallas kernels, per_device(): pl.pallas_call(finish, out_shape=(jax.ShapeDtypeStruct((ROWS, WIDTH), BF1...  2.18 us

profile of v5, /device:TPU:1, one launch (start us, length us, event | category | flops | bytes accessed | tf_op | source)
XLA Modules:
  0.0 44.6 jit_solution(17851044135449988635)
XLA Ops:
  0.6 41.7 %shard_map.59 = (bf16[1024,1024]{1,0:T(8,128)(2,1)S(1)}, f32[1024,1024]{1,0:T(8,128)S(1)}, bf16[1024,256]{1,0:T(8,128)(2,1)S(1)}, f32[2,32,1024]{2,1,0:T(8,128)S(1)}, f32[2,32,32]{2,1,0:T(8,128)S(1)}) custom-call(bf16[1440,1024]{1,0:T(8,128)(2,1)} %a_hbm.1, bf16[1440,2048]{1,0:T(8,128)(2,1)} %g_hbm.1, bf16[1024,2048]{1,0:T(8,128)(2,1)} %bitcast.8, ...), custom_call_target="tpu_custom_call" | custom-call | tf_op jit(solution)/shard_map/pallas_call | solution.py:316
  42.3 2.2 %shard_map.60 = (bf16[1024,2048]{1,0:T(8,128)(2,1)}, f32[64,1024]{1,0:T(8,128)}) custom-call(bf16[1024,1024]{1,0:T(8,128)(2,1)S(1)} %get-tuple-element.9.err0, f32[1024,1024]{1,0:T(8,128)S(1)} %get-tuple-element.10.mat1, bf16[1024,256]{1,0:T(8,128)(2,1)S(1)} %get-tuple-element.11.left1, f32[2,32,1024]{2,1,0:T(8,128)S(1)} %get-tuple-element.12.q_full, ...), custom_call_target="tpu_custom_call" | custom-call | tf_op jit(solution)/shard_map/pallas_call | solution.py:353
